TPU v7x, 128 devices: a whole 4x4x4 slice. The times are simulated.
128 devices in a mesh: user: 8 (over y_hi, z), item: 4 (over x), ctx: 4 (over y_lo, core).
Axes of the slice: x: 4, y: 4 (y_hi: 2, y_lo: 2; y = y_hi * 2 + y_lo), z: 4, core: 2. Of those that a mesh axis runs over, the one named last changes fastest.
Arguments:
- tile_values: bfloat16 [8, 4, 4, 16, 16, 128, 128], P('user', 'item', 'ctx'), may hold values from -127 to 127
- tile_weights: bfloat16 [8, 4, 4, 16, 16, 128, 128], P('user', 'item', 'ctx'), may hold values from 0 to 3
- tile_exponents: int32 [8, 4, 4, 16], P('user', 'item', 'ctx'), may hold values from -8 to -6
- tile_coords: int32 [8, 4, 4, 16, 3], P('user', 'item', 'ctx'), may hold values from 0 to 15, as said below
- tile_counts: int32 [8, 4, 4], P('user', 'item', 'ctx'), may hold values from 1 to 16, as said below
- user_factor: bfloat16 [8192, 256], P(('user', 'item', 'ctx')), may hold values from -2.5 to 2.5
- item_factor: bfloat16 [4096, 256], P(('item', 'user', 'ctx')), may hold values from -2.5 to 2.5
- context_factor: bfloat16 [1024, 256], P(('ctx', 'user', 'item')), may hold values from -2.5 to 2.5
Outputs:
- user_grad: float32 [8192, 256], P(('user', 'item', 'ctx'))
- item_grad: float32 [4096, 256], P(('item', 'user', 'ctx'))
- context_grad: float32 [1024, 256], P(('ctx', 'user', 'item'))
Inputs may be any that keep to these rules, and one draw needn't show every extreme that they name: `tile_coords`: per grid cell: tile numbers below 8, 8 and 16 for the three columns, no two slots of a cell at the same tile. `tile_counts`: some grid cell has all 16 slots live.
All inputs are finite; a program needn't handle non-finite values.
Results may differ from a plain program's by a relative error of at most 0.0012.
Values may be sent and summed in bfloat16 or wider, within the bound.
A program may use at most 64 MiB of HBM per device.

v0:
```python
import jax
import jax.numpy as jnp
from jax import lax
from jax.sharding import PartitionSpec as P


def tile_terms(a_rows, b_rows, g_rows, values, weights, exponent):
    scale = jnp.exp2(exponent.astype(jnp.float32))
    target = values.astype(jnp.float32) * scale
    depth, height, width = target.shape
    rank = a_rows.shape[1]
    product = (
        a_rows.astype(jnp.float32)[None, :, :] * g_rows.astype(jnp.float32)[:, None, :]
    ).astype(jnp.bfloat16)
    flat_ag = product.reshape(depth * height, rank)
    model = lax.dot_general(
        flat_ag, b_rows, (((1,), (1,)), ((), ())), preferred_element_type=jnp.float32
    )
    error = (
        weights.astype(jnp.float32).reshape(depth * height, width)
        * (model - target.reshape(depth * height, width))
    ).astype(jnp.bfloat16)
    proj = jnp.dot(error, b_rows, preferred_element_type=jnp.float32).reshape(depth, height, rank)
    user_term = jnp.sum(proj * g_rows.astype(jnp.float32)[:, None, :], axis=0)
    ctx_term = jnp.sum(proj * a_rows.astype(jnp.float32)[None, :, :], axis=1)
    item_term = lax.dot_general(
        error, flat_ag, (((0,), (0,)), ((), ())), preferred_element_type=jnp.float32
    )
    return (user_term, item_term, ctx_term)


def local(
    tile_values,
    tile_weights,
    tile_exponents,
    tile_coords,
    tile_counts,
    user_factor,
    item_factor,
    context_factor,
):
    user_block = lax.all_gather(user_factor, ("item", "ctx"), axis=0, tiled=True)
    item_block = lax.all_gather(item_factor, ("user", "ctx"), axis=0, tiled=True)
    ctx_block = lax.all_gather(context_factor, ("user", "item"), axis=0, tiled=True)
    values = tile_values[0, 0, 0]
    weights = tile_weights[0, 0, 0]
    exponents = tile_exponents[0, 0, 0]
    coords = tile_coords[0, 0, 0]
    count = tile_counts[0, 0, 0]
    slots, depth, height, width = values.shape

    def add_tile(slot, carry, live):
        grad_user, grad_item, grad_ctx = carry
        slot_coords = lax.dynamic_index_in_dim(coords, slot, 0, keepdims=False)
        user_row = slot_coords[0] * height
        item_row = slot_coords[1] * width
        ctx_row = slot_coords[2] * depth
        a_rows = lax.dynamic_slice_in_dim(user_block, user_row, height, 0)
        b_rows = lax.dynamic_slice_in_dim(item_block, item_row, width, 0)
        g_rows = lax.dynamic_slice_in_dim(ctx_block, ctx_row, depth, 0)
        slot_values = lax.dynamic_index_in_dim(values, slot, 0, keepdims=False)
        slot_weights = lax.dynamic_index_in_dim(weights, slot, 0, keepdims=False)
        slot_exp = lax.dynamic_index_in_dim(exponents, slot, 0, keepdims=False)
        user_term, item_term, ctx_term = tile_terms(
            a_rows, b_rows, g_rows, slot_values, slot_weights, slot_exp
        )
        zero = jnp.zeros((), jnp.int32)
        grad_user = lax.dynamic_update_slice(
            grad_user,
            lax.dynamic_slice_in_dim(grad_user, user_row, height, 0) + live * user_term,
            (user_row, zero),
        )
        grad_item = lax.dynamic_update_slice(
            grad_item,
            lax.dynamic_slice_in_dim(grad_item, item_row, width, 0) + live * item_term,
            (item_row, zero),
        )
        grad_ctx = lax.dynamic_update_slice(
            grad_ctx,
            lax.dynamic_slice_in_dim(grad_ctx, ctx_row, depth, 0) + live * ctx_term,
            (ctx_row, zero),
        )
        return (grad_user, grad_item, grad_ctx)

    init = (
        jnp.zeros(user_block.shape, jnp.float32),
        jnp.zeros(item_block.shape, jnp.float32),
        jnp.zeros(ctx_block.shape, jnp.float32),
    )

    def step(carry, slot):
        live = (slot < count).astype(jnp.float32)
        return (add_tile(slot, carry, live), None)

    totals, _ = lax.scan(step, init, jnp.arange(slots, dtype=jnp.int32))
    user_grad = lax.psum_scatter(totals[0], ("item", "ctx"), scatter_dimension=0, tiled=True)
    item_grad = lax.psum_scatter(totals[1], ("user", "ctx"), scatter_dimension=0, tiled=True)
    context_grad = lax.psum_scatter(totals[2], ("user", "item"), scatter_dimension=0, tiled=True)
    return (user_grad, item_grad, context_grad)


def solution(mesh):
    placed = (
        P("user", "item", "ctx", None, None, None, None),
        P("user", "item", "ctx", None, None, None, None),
        P("user", "item", "ctx", None),
        P("user", "item", "ctx", None, None),
        P("user", "item", "ctx"),
        P(("user", "item", "ctx"), None),
        P(("item", "user", "ctx"), None),
        P(("ctx", "user", "item"), None),
    )
    return jax.shard_map(
        local,
        mesh=mesh,
        in_specs=placed,
        out_specs=(
            P(("user", "item", "ctx"), None),
            P(("item", "user", "ctx"), None),
            P(("ctx", "user", "item"), None),
        ),
        check_vma=False,
    )
```

profile of v0, /device:TPU:1, one launch (start us, length us, event | category | flops | bytes accessed | tf_op | source)
XLA Modules:
  0.0 725.2 jit_solution(6212333429573216470)
XLA Ops:
  7.2 0.7 copy.13
  7.9 83.8 %all_gather.10 = bf16[256,256]{1,0:T(8,128)(2,1)S(1)} all-gather(bf16[8,256]{1,0:T(8,128)(2,1)} %param.17), channel_id=1, replica_groups=mesh['user'=8,'item'=4,'ctx'=4] {'user','item'}, dimensions={0}, use_global_device_ids=true | all-gather | bytes 135168 | tf_op jit(solution)/shard_map/all_gather | solution.py:44
  91.7 32.9 %all_gather.9 = bf16[1024,256]{1,0:T(8,128)(2,1)S(1)} all-gather(bf16[64,256]{1,0:T(8,128)(2,1)} %param.15), channel_id=1, replica_groups=mesh['user'=8,'item'=4,'ctx'=4] {'item','ctx'}, dimensions={0}, use_global_device_ids=true | all-gather | bytes 557056 | tf_op jit(solution)/shard_map/all_gather | solution.py:42
  124.5 38.1 %all_gather.11 = bf16[1024,256]{1,0:T(8,128)(2,1)S(1)} all-gather(bf16[32,256]{1,0:T(8,128)(2,1)} %param.16), channel_id=1, replica_groups=mesh['user'=8,'item'=4,'ctx'=4] {'user','ctx'}, dimensions={0}, use_global_device_ids=true | all-gather | bytes 540672 | tf_op jit(solution)/shard_map/all_gather | solution.py:43
  162.9 188.7 %while.14 = (s32[]{:T(128)}, f32[1024,256]{1,0:T(8,128)S(1)}, f32[1024,256]{1,0:T(8,128)S(1)}, f32[256,256]{1,0:T(8,128)S(1)}, s32[16]{0:T(128)S(1)}, /*index=5*...) while((s32[]{:T(128)}, f32[1024,256]{1,0:T(8,128)S(1)}, ...), condition=%wide.region_3.4_spmd, body=%wide.region_0.3_spmd.sunk | while | flops 407511040 | bytes 14606875 | solution.py:95
  168.1 0.6 fusion.27
  170.7 1.1 constant_dynamic-slice_fusion.5
  171.7 1.2 convert_multiply_fusion.2
  182.4 1.1 constant_dynamic-slice_fusion.5
  183.5 1.2 convert_multiply_fusion.2
  191.7 0.6 fusion.27
  194.2 1.1 constant_dynamic-slice_fusion.5
  195.3 1.2 convert_multiply_fusion.2
  203.4 0.6 fusion.27
  206.0 1.1 constant_dynamic-slice_fusion.5
  207.1 1.2 convert_multiply_fusion.2
  215.2 0.6 fusion.27
  217.8 1.1 constant_dynamic-slice_fusion.5
  218.9 1.2 convert_multiply_fusion.2
  227.0 0.6 fusion.27
  229.6 1.1 constant_dynamic-slice_fusion.5
  230.7 1.2 convert_multiply_fusion.2
  238.8 0.6 fusion.27
  241.4 1.1 constant_dynamic-slice_fusion.5
  242.5 1.2 convert_multiply_fusion.2
  253.2 1.1 constant_dynamic-slice_fusion.5
  254.3 1.2 convert_multiply_fusion.2
  265.0 1.1 constant_dynamic-slice_fusion.5
  266.1 1.2 convert_multiply_fusion.2
  276.8 1.1 constant_dynamic-slice_fusion.5
  277.9 1.2 convert_multiply_fusion.2
  288.6 1.1 constant_dynamic-slice_fusion.5
  289.7 1.2 convert_multiply_fusion.2
  300.4 1.1 constant_dynamic-slice_fusion.5
  301.5 1.2 convert_multiply_fusion.2
  312.2 1.1 constant_dynamic-slice_fusion.5
  313.3 1.2 convert_multiply_fusion.2
  324.0 1.1 constant_dynamic-slice_fusion.5
  325.1 1.2 convert_multiply_fusion.2
  335.8 1.1 constant_dynamic-slice_fusion.5
  336.9 1.2 convert_multiply_fusion.2
  347.6 1.1 constant_dynamic-slice_fusion.5
  348.7 1.2 convert_multiply_fusion.2
  351.7 0.7 copy-done.2
  353.2 0.7 reduce-scatter.6.cloned.1.call-update
  353.9 150.1 %reduce-scatter.8.cloned.1.call-done = f32[8,256]{1,0:T(8,128)} async-done(((f32[256,256]{1,0:T(8,128)}), f32[8,256]{1,0:T(8,128)}) %reduce-scatter.8.cloned.1.call-update) | async-done | bytes 8208 | tf_op jit(solution)/shard_map/reduce_scatter | solution.py:98
  504.0 81.5 %reduce-scatter.4.cloned.1.call-done = f32[64,256]{1,0:T(8,128)} async-done(((f32[1024,256]{1,0:T(8,128)}), f32[64,256]{1,0:T(8,128)}) %reduce-scatter.4.cloned.1.call-update) | async-done | bytes 65552 | tf_op jit(solution)/shard_map/reduce_scatter | solution.py:96
  585.4 133.2 %reduce-scatter.6.cloned.1.call-done = f32[32,256]{1,0:T(8,128)} async-done(((f32[1024,256]{1,0:T(8,128)}), f32[32,256]{1,0:T(8,128)}) %reduce-scatter.6.cloned.1.call-update) | async-done | bytes 32784 | tf_op jit(solution)/shard_map/reduce_scatter | solution.py:97
  (218 shorter events, 54.8 us)
Async XLA Ops:
  7.2 155.7 %copy-start.3 = (s32[1,1,1,16]{3,2,1,0:T(1,128)S(1)}, s32[1,1,1,16]{3,2,1,0:T(1,128)}, u32[]{:S(2)}) copy-start(s32[1,1,1,16]{3,2,1,0:T(1,128)} %param.12) | copy-start | bytes 196
  7.2 496.8 %reduce-scatter.8.cloned.1.call-start = ((), (), s32[]{:S(2)}) async-start(), calls=%async_computation.5 | async-start | bytes 270336 | tf_op jit(solution)/shard_map/reduce_scatter | solution.py:98
  351.6 0.7 copy-start.2
  351.6 1.1 copy-start.1
  351.7 1.5 copy-start
  352.4 233.0 %reduce-scatter.4.cloned.1.call-start = ((), (), s32[]{:S(2)}) async-start(), calls=%async_computation.3 | async-start | bytes 1114112 | tf_op jit(solution)/shard_map/reduce_scatter | solution.py:96
  353.1 365.5 %reduce-scatter.6.cloned.1.call-start = ((), (), s32[]{:S(2)}) async-start(), calls=%async_computation.4 | async-start | bytes 1081344 | tf_op jit(solution)/shard_map/reduce_scatter | solution.py:97
Sparse Core Ops, SparseCore 0:
  352.5 151.4 reduce-scatter.7
  507.0 78.3 reduce-scatter.3
  588.3 130.2 reduce-scatter.5
where the time goes:
time: 732 us; the launch traced here: 725 us
  waiting for transfers between devices  366 us (50%)
  blocking collectives  155 us (21%)
  loops' own time  95.6 us (13%)
  local copies, waits for them, and re-layouts  48.6 us (7%)
  other arithmetic  26 us (4%)
  matrix products  20.4 us (3%)
  between operations  13.8 us (2%)
    reduce_scatter x1, waiting for transfers between devices, local(): lax.psum_scatter(totals[2], ('user', 'item'), scatter_dimension=0, tiled=...  150 us
    reduce_scatter x1, waiting for transfers between devices, local(): lax.psum_scatter(totals[1], ('user', 'ctx'), scatter_dimension=0, tiled=T...  133 us
    another operation x1, loops' own time, local(): totals, _ = lax.scan(step, init, jnp.arange(slots, dtype=jnp.int32))  95.6 us
    all_gather x1, blocking collectives, local(): lax.all_gather(context_factor, ('user', 'item'), axis=0, tiled=True)  83.8 us
    reduce_scatter x1, waiting for transfers between devices, local(): lax.psum_scatter(totals[0], ('item', 'ctx'), scatter_dimension=0, tiled=T...  81.5 us
    all_gather x1, blocking collectives, local(): lax.all_gather(item_factor, ('user', 'ctx'), axis=0, tiled=True)  38.1 us
    all_gather x1, blocking collectives, local(): lax.all_gather(user_factor, ('item', 'ctx'), axis=0, tiled=True)  32.9 us
    mul x16, other arithmetic, tile_terms(): target = values.astype(jnp.float32) * scale  18.4 us
  transfers between devices with their start and end apart: 3, of which 3 were waited for; matrix products, arithmetic and copies ran while one was open for 0% of the time, Pallas kernels for 0%

commit v1 on v0

v1 whole, which is shorter than its diff:
```python
import functools

import jax
import jax.numpy as jnp
from jax import lax
from jax.experimental import pallas as pl
from jax.experimental.pallas import tpu as pltpu
from jax.sharding import PartitionSpec as P

MESH = pl.DeviceIdType.MESH
F32 = jnp.float32
BF16 = jnp.bfloat16
SLOTS, DEPTH, TU, TI, RANK = 16, 16, 128, 128, 256
UT, IT, CT = 8, 8, 16
NU, NI, NC = 8, 4, 4


def copy_to(src, dst, send, recv, device):
    return pltpu.make_async_remote_copy(
        src_ref=src,
        dst_ref=dst,
        send_sem=send,
        recv_sem=recv,
        device_id=device,
        device_id_type=MESH,
    )


def wait_bytes(ref, sem):
    pltpu.make_async_copy(ref, ref, sem).wait()


def kernel(
    values,
    weights,
    exps,
    coords,
    counts,
    uf,
    itf,
    cf,
    ug_out,
    ig_out,
    cg_out,
    vbuf,
    wbuf,
    ublk,
    iblk,
    cstage,
    cblk,
    gblk,
    ags,
    errs,
    iterms,
    uterms,
    cterms,
    prev,
    last,
    usum,
    isum,
    csum,
    umate,
    imate,
    urecv,
    irecv,
    crecv,
    load_sem,
    gsend,
    grecv,
    rsend,
    rrecv,
):
    u = lax.axis_index("user")
    i = lax.axis_index("item")
    c = lax.axis_index("ctx")
    ylo = c // 2
    core = c % 2
    mate = (u, i, ylo * 2 + 1 - core)
    uj = i * 2 + ylo
    ij = u * 2 + ylo
    cj = u * 4 + i

    def load(slot):
        return (
            pltpu.make_async_copy(
                values.at[0, 0, 0, slot], vbuf.at[slot], load_sem.at[0, slot]
            ),
            pltpu.make_async_copy(
                weights.at[0, 0, 0, slot], wbuf.at[slot], load_sem.at[1, slot]
            ),
        )

    def start_load(slot, carry):
        for copy in load(slot):
            copy.start()
        return carry

    lax.fori_loop(0, SLOTS, start_load, 0)

    def user_peer(d):
        j = (uj + d) % 8
        return (u, j // 2, (j % 2) * 2 + core)

    def item_peer(d):
        j = (ij + d) % 16
        return (j // 2, i, (j % 2) * 2 + core)

    def ctx_peer(d):
        j = (cj + d) % 32
        return (j // 4, j % 4, c)

    barrier = pltpu.get_barrier_semaphore()

    def greet(peer, n):
        def one(d, carry):
            pl.semaphore_signal(barrier, inc=1, device_id=peer(d), device_id_type=MESH)
            return carry

        lax.fori_loop(1, n, one, 0)

    greet(user_peer, 8)
    greet(item_peer, 16)
    greet(ctx_peer, 32)
    pl.semaphore_signal(barrier, inc=1, device_id=mate, device_id_type=MESH)

    ublk[core, uj] = uf[...]
    iblk[core, ij] = itf[...]
    own = cf[...].astype(F32)
    cstage[...] = jnp.concatenate([own[:, :128], own[:, 128:]], axis=0).astype(BF16)
    cblk[cj] = cstage[...]

    pl.semaphore_wait(barrier, 7 + 15 + 31 + 1)

    def gather_user(d, carry):
        copy_to(uf, ublk.at[core, uj], gsend.at[0], grecv.at[0], user_peer(d)).start()
        return carry

    def gather_item(d, carry):
        copy_to(itf, iblk.at[core, ij], gsend.at[1], grecv.at[1], item_peer(d)).start()
        return carry

    def gather_ctx(d, carry):
        copy_to(cstage, cblk.at[cj], gsend.at[2], grecv.at[2], ctx_peer(d)).start()
        return carry

    lax.fori_loop(1, 16, gather_item, 0)
    lax.fori_loop(1, 8, gather_user, 0)
    lax.fori_loop(1, 32, gather_ctx, 0)

    count = counts[0, 0, 0]
    tile = [[coords[0, 0, 0, s, m] for s in range(SLOTS)] for m in range(3)]
    for m in range(3):
        for s in range(SLOTS):
            entry = jnp.int32(0)
            for t in range(s):
                entry = jnp.where(tile[m][t] == tile[m][s], t + 1, entry)
            prev[m, s] = entry
        for n in range((UT, IT, CT)[m]):
            entry = jnp.int32(0)
            for s in range(SLOTS):
                hit = jnp.logical_and(tile[m][s] == n, s < count)
                entry = jnp.where(hit, s + 1, entry)
            last[m, n] = entry
    iterms[0] = jnp.zeros((TI, RANK), F32)
    uterms[0] = jnp.zeros((TU, RANK), F32)
    cterms[0] = jnp.zeros((DEPTH, RANK), F32)

    wait_bytes(iblk.at[0, pl.ds(0, 15)], grecv.at[1])
    item_forward = copy_to(
        iblk.at[core], iblk.at[core], gsend.at[3], grecv.at[3], mate
    )
    item_forward.start()
    wait_bytes(ublk.at[0, pl.ds(0, 7)], grecv.at[0])
    user_forward = copy_to(
        ublk.at[core], ublk.at[core], gsend.at[4], grecv.at[4], mate
    )
    user_forward.start()
    wait_bytes(cblk.at[pl.ds(0, 31)], grecv.at[2])

    def unpack_ctx(t, carry):
        rows = []
        for half in range(2):
            pair = cblk[2 * t + half].astype(F32)
            rows.append(jnp.concatenate([pair[:8], pair[8:]], axis=1))
        gblk[t] = jnp.concatenate(rows, axis=0)
        return carry

    lax.fori_loop(0, CT, unpack_ctx, 0)
    item_forward.wait()
    user_forward.wait()
    wait_bytes(ublk.at[0, pl.ds(0, 7)], gsend.at[0])
    wait_bytes(iblk.at[0, pl.ds(0, 15)], gsend.at[1])
    wait_bytes(cblk.at[pl.ds(0, 31)], gsend.at[2])

    def user_rows(slot):
        t = coords[0, 0, 0, slot, 0]
        return jnp.concatenate([ublk[0, t], ublk[1, t]], axis=0)

    def item_rows(slot):
        t = coords[0, 0, 0, slot, 1]
        return jnp.concatenate(
            [
                iblk[0, 2 * t],
                iblk[1, 2 * t],
                iblk[0, 2 * t + 1],
                iblk[1, 2 * t + 1],
            ],
            axis=0,
        )

    step = 2

    def phase_a(slot, carry):
        for copy in load(slot):
            copy.wait()
        a = user_rows(slot)
        b = item_rows(slot)
        g = gblk[coords[0, 0, 0, slot, 2]].astype(BF16)
        scale = lax.shift_left(jnp.int32(1), exps[0, 0, 0, slot] + 30).astype(F32) * (
            2.0**-30
        )
        for k in range(0, DEPTH, step):
            rows = pl.ds(k * TU, step * TU)
            ag = (a[None] * g[k : k + step][:, None, :]).reshape(step * TU, RANK)
            ags[rows] = ag
            model = lax.dot_general(
                ag, b, (((1,), (1,)), ((), ())), preferred_element_type=F32
            )
            w = wbuf[slot, k : k + step].reshape(step * TU, TI).astype(F32)
            v = vbuf[slot, k : k + step].reshape(step * TU, TI).astype(F32)
            errs[slot, rows] = (w * (model - v * scale)).astype(BF16)
        term = lax.dot_general(
            errs[slot], ags[...], (((0,), (0,)), ((), ())), preferred_element_type=F32
        )
        iterms[slot + 1] = term + iterms[prev[1, slot]]
        return carry

    def phase_b(slot, carry):
        a = user_rows(slot).astype(F32)
        b = item_rows(slot)
        g = gblk[coords[0, 0, 0, slot, 2]]
        total = uterms[prev[0, slot]]
        rows = []
        for k in range(DEPTH):
            proj = jnp.dot(
                errs[slot, pl.ds(k * TU, TU)], b, preferred_element_type=F32
            )
            total = total + proj * g[k : k + 1]
            rows.append(jnp.sum(proj * a, axis=0, keepdims=True))
        uterms[slot + 1] = total
        cterms[slot + 1] = jnp.concatenate(rows, axis=0) + cterms[prev[2, slot]]
        return carry

    lax.fori_loop(0, SLOTS, phase_a, 0)
    lax.fori_loop(0, SLOTS, phase_b, 0)

    for t in range(UT):
        rows = uterms[last[0, t]]
        usum[0, t] = rows[:64]
        usum[1, t] = rows[64:]
    user_mate = copy_to(
        usum.at[1 - core], umate, rsend.at[0], rrecv.at[0], mate
    )
    user_mate.start()
    for t in range(IT):
        rows = iterms[last[1, t]]
        isum[0, 2 * t] = rows[:32]
        isum[1, 2 * t] = rows[32:64]
        isum[0, 2 * t + 1] = rows[64:96]
        isum[1, 2 * t + 1] = rows[96:]
    item_mate = copy_to(
        isum.at[1 - core], imate, rsend.at[1], rrecv.at[1], mate
    )
    item_mate.start()
    for t in range(CT):
        rows = cterms[last[2, t]]
        csum[2 * t] = rows[:8]
        csum[2 * t + 1] = rows[8:]
    crecv[cj] = csum[cj]

    def scatter_ctx(d, carry):
        j = (cj + d) % 32
        copy_to(csum.at[j], crecv.at[cj], rsend.at[4], rrecv.at[4], ctx_peer(d)).start()
        return carry

    lax.fori_loop(1, 32, scatter_ctx, 0)

    user_mate.wait()
    for j in range(8):
        umate[j] += usum[core, j]
    urecv[uj] = umate[uj]

    def scatter_user(d, carry):
        j = (uj + d) % 8
        copy_to(umate.at[j], urecv.at[uj], rsend.at[2], rrecv.at[2], user_peer(d)).start()
        return carry

    lax.fori_loop(1, 8, scatter_user, 0)

    item_mate.wait()
    for j in range(16):
        imate[j] += isum[core, j]
    irecv[ij] = imate[ij]

    def scatter_item(d, carry):
        j = (ij + d) % 16
        copy_to(imate.at[j], irecv.at[ij], rsend.at[3], rrecv.at[3], item_peer(d)).start()
        return carry

    lax.fori_loop(1, 16, scatter_item, 0)

    wait_bytes(crecv.at[pl.ds(0, 31)], rrecv.at[4])
    cg_out[...] = jnp.sum(crecv[...], axis=0)
    wait_bytes(urecv.at[pl.ds(0, 7)], rrecv.at[2])
    ug_out[...] = jnp.sum(urecv[...], axis=0)
    wait_bytes(irecv.at[pl.ds(0, 15)], rrecv.at[3])
    ig_out[...] = jnp.sum(irecv[...], axis=0)
    wait_bytes(urecv.at[pl.ds(0, 7)], rsend.at[2])
    wait_bytes(irecv.at[pl.ds(0, 15)], rsend.at[3])
    wait_bytes(crecv.at[pl.ds(0, 31)], rsend.at[4])


def local(
    values,
    weights,
    exps,
    coords,
    counts,
    uf,
    itf,
    cf,
):
    hbm = pl.BlockSpec(memory_space=pltpu.HBM)
    smem = pl.BlockSpec(memory_space=pltpu.SMEM)
    vmem = pl.BlockSpec(memory_space=pltpu.VMEM)
    dma = pltpu.SemaphoreType.DMA
    return pl.pallas_call(
        kernel,
        in_specs=[hbm, hbm, smem, smem, smem, vmem, vmem, vmem],
        out_specs=[vmem, vmem, vmem],
        out_shape=[
            jax.ShapeDtypeStruct(uf.shape, F32),
            jax.ShapeDtypeStruct(itf.shape, F32),
            jax.ShapeDtypeStruct(cf.shape, F32),
        ],
        scratch_shapes=[
            pltpu.VMEM((SLOTS, DEPTH, TU, TI), BF16),
            pltpu.VMEM((SLOTS, DEPTH, TU, TI), BF16),
            pltpu.VMEM((2, 8, 64, RANK), BF16),
            pltpu.VMEM((2, 16, 32, RANK), BF16),
            pltpu.VMEM((16, 128), BF16),
            pltpu.VMEM((32, 16, 128), BF16),
            pltpu.VMEM((CT, DEPTH, RANK), F32),
            pltpu.VMEM((DEPTH * TU, RANK), BF16),
            pltpu.VMEM((SLOTS, DEPTH * TU, TI), BF16),
            pltpu.VMEM((SLOTS + 1, TI, RANK), F32),
            pltpu.VMEM((SLOTS + 1, TU, RANK), F32),
            pltpu.VMEM((SLOTS + 1, DEPTH, RANK), F32),
            pltpu.SMEM((3, SLOTS), jnp.int32),
            pltpu.SMEM((3, CT), jnp.int32),
            pltpu.VMEM((2, 8, 64, RANK), F32),
            pltpu.VMEM((2, 16, 32, RANK), F32),
            pltpu.VMEM((32, 8, RANK), F32),
            pltpu.VMEM((8, 64, RANK), F32),
            pltpu.VMEM((16, 32, RANK), F32),
            pltpu.VMEM((8, 64, RANK), F32),
            pltpu.VMEM((16, 32, RANK), F32),
            pltpu.VMEM((32, 8, RANK), F32),
            dma((2, SLOTS)),
            dma((5,)),
            dma((5,)),
            dma((5,)),
            dma((5,)),
        ],
        compiler_params=pltpu.CompilerParams(
            collective_id=0,
            has_side_effects=True,
            vmem_limit_bytes=56 * 2**20,
        ),
        name="cp_gradient",
    )(values, weights, exps, coords, counts, uf, itf, cf)


def solution(mesh):
    placed = (
        P("user", "item", "ctx", None, None, None, None),
        P("user", "item", "ctx", None, None, None, None),
        P("user", "item", "ctx", None),
        P("user", "item", "ctx", None, None),
        P("user", "item", "ctx"),
        P(("user", "item", "ctx"), None),
        P(("item", "user", "ctx"), None),
        P(("ctx", "user", "item"), None),
    )
    return jax.shard_map(
        local,
        mesh=mesh,
        in_specs=placed,
        out_specs=(
            P(("user", "item", "ctx"), None),
            P(("item", "user", "ctx"), None),
            P(("ctx", "user", "item"), None),
        ),
        check_vma=False,
    )
```

time: 732 us -> 69.7 us (0.10)
  waiting for transfers between devices: 366 us -> 0 us
  blocking collectives: 155 us -> 0 us
  loops' own time: 95.6 us -> 0 us
  Pallas kernels: 0 us -> 62.6 us
  local copies, waits for them, and re-layouts: 48.6 us -> 5.5 us
  other arithmetic: 26 us -> 0 us
  matrix products: 20.4 us -> 0 us
  between operations: 13.8 us -> 1.29 us
    reduce_scatter x3 -> x0, waiting for transfers between devices: 365 us -> none  [the longest x1 150 us: local(): lax.psum_scatter(totals[2], ('user', 'item'), scatter_dimension=0, tiled=...]
    all_gather x3 -> x0, blocking collectives: 155 us -> none  [the longest x1 83.8 us: local(): lax.all_gather(context_factor, ('user', 'item'), axis=0, tiled=True)]
    another operation x1 -> x0, loops' own time: 95.6 us -> none  [local(): totals, _ = lax.scan(step, init, jnp.arange(slots, dtype=jnp.int32))]
    pallas_call x0 -> x1, Pallas kernels: none -> 62.6 us  [local(): pl.pallas_call(kernel, in_specs=[hbm, hbm, smem, smem, smem, vmem, vmem,...]
    dynamic_slice x64 -> x0, local copies, waits for them, and re-layouts: 37.4 us -> none  [the longest x16 17.4 us: add_tile(): slot_weights = lax.dynamic_index_in_dim(weights, slot, 0, keepdims=False)]
    dot_general x48 -> x0, matrix products: 20.4 us -> none  [the longest x16 7.1 us: tile_terms(): lax.dot_general(flat_ag, b_rows, (((1,), (1,)), ((), ())), preferred_elem...]
    mul x16 -> x0, other arithmetic: 18.4 us -> none  [tile_terms(): target = values.astype(jnp.float32) * scale]
    slice x16 -> x0, local copies, waits for them, and re-layouts: 9.41 us -> none  [add_tile(): item_row = slot_coords[1] * width]
  transfers between devices with their start and end apart: 3 -> 0, of which waited for: 3 -> 0; matrix products, arithmetic and copies ran while one was open for 0% -> 0% of each run, Pallas kernels for 0% -> 0%
where the time goes in v1:
time: 69.7 us; the launch traced here: 69.3 us
  Pallas kernels  62.6 us (90%)
  local copies, waits for them, and re-layouts  5.5 us (8%)
  between operations  1.29 us (2%)
    pallas_call x1, Pallas kernels, local(): pl.pallas_call(kernel, in_specs=[hbm, hbm, smem, smem, smem, vmem, vmem,...  62.6 us
    unnamed x4, local copies, waits for them, and re-layouts  5.5 us

profile of v1, /device:TPU:1, one launch (start us, length us, event | category | flops | bytes accessed | tf_op | source)
XLA Modules:
  0.0 69.3 jit_solution(5932562379015075731)
XLA Ops:
  1.3 1.4 %copy.11.coords = s32[1,1,1,16,3]{4,3,2,1,0:T(8,128)} copy(s32[1,1,1,16,3]{3,2,4,1,0:T(1,128)} %param.11) | data formatting | bytes 384 | tf_op args[3]
  2.6 62.6 %cp_gradient.1 = (f32[64,256]{1,0:T(8,128)}, f32[32,256]{1,0:T(8,128)}, f32[8,256]{1,0:T(8,128)}) custom-call(bf16[1,1,1,16,16,128,128]{6,5,4,3,2,1,0:T(8,128)(2,1)} %values.1, bf16[1,1,1,16,16,128,128]{6,5,4,3,2,1,0:T(8,128)(2,1)} %weights.1, s32[1,1,1,16]{3,2,1,0:T(1,128)} %exps.1, s32[1,1,1,16,3]{4,3,2,1,0:T(8,128)} %copy.11.coords, ...), custom_call_target="tpu_custom_call" | custom-call | tf_op jit(solution)/shard_map/cp_gradient/pallas_call | solution.py:337
  65.2 1.5 %copy.16 = f32[64,256]{1,0:T(8,128)} copy(f32[64,256]{1,0:T(8,128)} %get-tuple-element.6) | data formatting | bytes 131072
  66.7 1.4 %copy.17 = f32[32,256]{1,0:T(8,128)} copy(f32[32,256]{1,0:T(8,128)} %get-tuple-element.7) | data formatting | bytes 65536
  68.0 1.3 %copy.18 = f32[8,256]{1,0:T(8,128)} copy(f32[8,256]{1,0:T(8,128)} %get-tuple-element.8) | data formatting | bytes 16384

commit v2 on v1

--- a/solution.py
+++ b/solution.py
@@ -49,7 +49,6 @@
     cstage,
     cblk,
     gblk,
-    ags,
     errs,
     iterms,
     uterms,
@@ -148,7 +147,7 @@
     lax.fori_loop(1, 32, gather_ctx, 0)
 
     count = counts[0, 0, 0]
-    tile = [[coords[0, 0, 0, s, m] for s in range(SLOTS)] for m in range(3)]
+    tile = [[coords[0, 0, m, 0, s] for s in range(SLOTS)] for m in range(3)]
     for m in range(3):
         for s in range(SLOTS):
             entry = jnp.int32(0)
@@ -162,8 +161,9 @@
                 entry = jnp.where(hit, s + 1, entry)
             last[m, n] = entry
     iterms[0] = jnp.zeros((TI, RANK), F32)
-    uterms[0] = jnp.zeros((TU, RANK), F32)
-    cterms[0] = jnp.zeros((DEPTH, RANK), F32)
+    for order in range(2):
+        uterms[order, 0] = jnp.zeros((64, RANK), F32)
+        cterms[order, 0] = jnp.zeros((DEPTH, RANK), F32)
 
     wait_bytes(iblk.at[0, pl.ds(0, 15)], grecv.at[1])
     item_forward = copy_to(
@@ -192,12 +192,8 @@
     wait_bytes(iblk.at[0, pl.ds(0, 15)], gsend.at[1])
     wait_bytes(cblk.at[pl.ds(0, 31)], gsend.at[2])
 
-    def user_rows(slot):
-        t = coords[0, 0, 0, slot, 0]
-        return jnp.concatenate([ublk[0, t], ublk[1, t]], axis=0)
-
     def item_rows(slot):
-        t = coords[0, 0, 0, slot, 1]
+        t = coords[0, 0, 1, 0, slot]
         return jnp.concatenate(
             [
                 iblk[0, 2 * t],
@@ -208,94 +204,75 @@
             axis=0,
         )
 
-    step = 2
-
-    def phase_a(slot, carry):
+    step = 4
+
+    def end_load(slot, carry):
         for copy in load(slot):
             copy.wait()
-        a = user_rows(slot)
+        return carry
+
+    lax.fori_loop(0, SLOTS, end_load, 0)
+
+    def phase_a(slot, carry):
+        t = coords[0, 0, 0, 0, slot]
+        a = jnp.concatenate([ublk[0, t], ublk[1, t]], axis=0)
         b = item_rows(slot)
-        g = gblk[coords[0, 0, 0, slot, 2]].astype(BF16)
+        g = gblk[coords[0, 0, 2, 0, slot]].astype(BF16)
         scale = lax.shift_left(jnp.int32(1), exps[0, 0, 0, slot] + 30).astype(F32) * (
             2.0**-30
         )
+        term = jnp.zeros((TI, RANK), F32)
         for k in range(0, DEPTH, step):
-            rows = pl.ds(k * TU, step * TU)
             ag = (a[None] * g[k : k + step][:, None, :]).reshape(step * TU, RANK)
-            ags[rows] = ag
             model = lax.dot_general(
                 ag, b, (((1,), (1,)), ((), ())), preferred_element_type=F32
             )
             w = wbuf[slot, k : k + step].reshape(step * TU, TI).astype(F32)
             v = vbuf[slot, k : k + step].reshape(step * TU, TI).astype(F32)
-            errs[slot, rows] = (w * (model - v * scale)).astype(BF16)
-        term = lax.dot_general(
-            errs[slot], ags[...], (((0,), (0,)), ((), ())), preferred_element_type=F32
-        )
+            err = (w * (model - v * scale)).astype(BF16)
+            for n in range(step):
+                errs[slot, 0, k + n] = err[n * TU : n * TU + 64]
+                errs[slot, 1, k + n] = err[n * TU + 64 : n * TU + TU]
+            term = term + lax.dot_general(
+                err, ag, (((0,), (0,)), ((), ())), preferred_element_type=F32
+            )
         iterms[slot + 1] = term + iterms[prev[1, slot]]
         return carry
 
-    def phase_b(slot, carry):
-        a = user_rows(slot).astype(F32)
+    def phase_b(order, slot, carry):
+        half = core if order else 1 - core
+        a = ublk[half, coords[0, 0, 0, 0, slot]].astype(F32)
         b = item_rows(slot)
-        g = gblk[coords[0, 0, 0, slot, 2]]
-        total = uterms[prev[0, slot]]
+        g = gblk[coords[0, 0, 2, 0, slot]]
+        total = jnp.zeros((64, RANK), F32)
         rows = []
         for k in range(DEPTH):
-            proj = jnp.dot(
-                errs[slot, pl.ds(k * TU, TU)], b, preferred_element_type=F32
-            )
+            proj = jnp.dot(errs[slot, half, k], b, preferred_element_type=F32)
             total = total + proj * g[k : k + 1]
             rows.append(jnp.sum(proj * a, axis=0, keepdims=True))
-        uterms[slot + 1] = total
-        cterms[slot + 1] = jnp.concatenate(rows, axis=0) + cterms[prev[2, slot]]
-        return carry
-
-    lax.fori_loop(0, SLOTS, phase_a, 0)
-    lax.fori_loop(0, SLOTS, phase_b, 0)
-
-    for t in range(UT):
-        rows = uterms[last[0, t]]
-        usum[0, t] = rows[:64]
-        usum[1, t] = rows[64:]
-    user_mate = copy_to(
-        usum.at[1 - core], umate, rsend.at[0], rrecv.at[0], mate
-    )
-    user_mate.start()
+        uterms[order, slot + 1] = total + uterms[order, prev[0, slot]]
+        cterms[order, slot + 1] = (
+            jnp.concatenate(rows, axis=0) + cterms[order, prev[2, slot]]
+        )
+        return carry
+
+    lax.fori_loop(0, SLOTS, phase_a, 0, unroll=4)
+
     for t in range(IT):
         rows = iterms[last[1, t]]
         isum[0, 2 * t] = rows[:32]
         isum[1, 2 * t] = rows[32:64]
         isum[0, 2 * t + 1] = rows[64:96]
         isum[1, 2 * t + 1] = rows[96:]
-    item_mate = copy_to(
-        isum.at[1 - core], imate, rsend.at[1], rrecv.at[1], mate
-    )
+    item_mate = copy_to(isum.at[1 - core], imate, rsend.at[1], rrecv.at[1], mate)
     item_mate.start()
-    for t in range(CT):
-        rows = cterms[last[2, t]]
-        csum[2 * t] = rows[:8]
-        csum[2 * t + 1] = rows[8:]
-    crecv[cj] = csum[cj]
-
-    def scatter_ctx(d, carry):
-        j = (cj + d) % 32
-        copy_to(csum.at[j], crecv.at[cj], rsend.at[4], rrecv.at[4], ctx_peer(d)).start()
-        return carry
-
-    lax.fori_loop(1, 32, scatter_ctx, 0)
-
-    user_mate.wait()
-    for j in range(8):
-        umate[j] += usum[core, j]
-    urecv[uj] = umate[uj]
-
-    def scatter_user(d, carry):
-        j = (uj + d) % 8
-        copy_to(umate.at[j], urecv.at[uj], rsend.at[2], rrecv.at[2], user_peer(d)).start()
-        return carry
-
-    lax.fori_loop(1, 8, scatter_user, 0)
+
+    lax.fori_loop(0, SLOTS, functools.partial(phase_b, 0), 0, unroll=4)
+
+    for t in range(UT):
+        usum[t] = uterms[0, last[0, t]]
+    user_mate = copy_to(usum, umate, rsend.at[0], rrecv.at[0], mate)
+    user_mate.start()
 
     item_mate.wait()
     for j in range(16):
@@ -309,15 +286,48 @@
 
     lax.fori_loop(1, 16, scatter_item, 0)
 
+    lax.fori_loop(0, SLOTS, functools.partial(phase_b, 1), 0, unroll=4)
+
+    user_mate.wait()
+    for t in range(UT):
+        umate[t] += uterms[1, last[0, t]]
+    urecv[uj] = umate[uj]
+
+    def scatter_user(d, carry):
+        j = (uj + d) % 8
+        copy_to(umate.at[j], urecv.at[uj], rsend.at[2], rrecv.at[2], user_peer(d)).start()
+        return carry
+
+    lax.fori_loop(1, 8, scatter_user, 0)
+
+    for t in range(CT):
+        rows = cterms[0, last[2, t]] + cterms[1, last[2, t]]
+        csum[2 * t] = rows[:8]
+        csum[2 * t + 1] = rows[8:]
+    crecv[cj] = csum[cj]
+
+    def scatter_ctx(d, carry):
+        j = (cj + d) % 32
+        copy_to(csum.at[j], crecv.at[cj], rsend.at[4], rrecv.at[4], ctx_peer(d)).start()
+        return carry
+
+    lax.fori_loop(1, 32, scatter_ctx, 0)
+
+    wait_bytes(irecv.at[pl.ds(0, 15)], rrecv.at[3])
+    ig_out[...] = jnp.sum(irecv[...], axis=0)
+    wait_bytes(urecv.at[pl.ds(0, 7)], rrecv.at[2])
+    ug_out[...] = jnp.sum(urecv[...], axis=0)
     wait_bytes(crecv.at[pl.ds(0, 31)], rrecv.at[4])
     cg_out[...] = jnp.sum(crecv[...], axis=0)
-    wait_bytes(urecv.at[pl.ds(0, 7)], rrecv.at[2])
-    ug_out[...] = jnp.sum(urecv[...], axis=0)
-    wait_bytes(irecv.at[pl.ds(0, 15)], rrecv.at[3])
-    ig_out[...] = jnp.sum(irecv[...], axis=0)
     wait_bytes(urecv.at[pl.ds(0, 7)], rsend.at[2])
     wait_bytes(irecv.at[pl.ds(0, 15)], rsend.at[3])
     wait_bytes(crecv.at[pl.ds(0, 31)], rsend.at[4])
+
+
+def copy_out(ug, ig, cg, ug_out, ig_out, cg_out):
+    ug_out[...] = ug[...]
+    ig_out[...] = ig[...]
+    cg_out[...] = cg[...]
 
 
 def local(
@@ -334,7 +344,7 @@
     smem = pl.BlockSpec(memory_space=pltpu.SMEM)
     vmem = pl.BlockSpec(memory_space=pltpu.VMEM)
     dma = pltpu.SemaphoreType.DMA
-    return pl.pallas_call(
+    grads = pl.pallas_call(
         kernel,
         in_specs=[hbm, hbm, smem, smem, smem, vmem, vmem, vmem],
         out_specs=[vmem, vmem, vmem],
@@ -351,14 +361,13 @@
             pltpu.VMEM((16, 128), BF16),
             pltpu.VMEM((32, 16, 128), BF16),
             pltpu.VMEM((CT, DEPTH, RANK), F32),
-            pltpu.VMEM((DEPTH * TU, RANK), BF16),
-            pltpu.VMEM((SLOTS, DEPTH * TU, TI), BF16),
+            pltpu.VMEM((SLOTS, 2, DEPTH, 64, TI), BF16),
             pltpu.VMEM((SLOTS + 1, TI, RANK), F32),
-            pltpu.VMEM((SLOTS + 1, TU, RANK), F32),
-            pltpu.VMEM((SLOTS + 1, DEPTH, RANK), F32),
+            pltpu.VMEM((2, SLOTS + 1, 64, RANK), F32),
+            pltpu.VMEM((2, SLOTS + 1, DEPTH, RANK), F32),
             pltpu.SMEM((3, SLOTS), jnp.int32),
             pltpu.SMEM((3, CT), jnp.int32),
-            pltpu.VMEM((2, 8, 64, RANK), F32),
+            pltpu.VMEM((8, 64, RANK), F32),
             pltpu.VMEM((2, 16, 32, RANK), F32),
             pltpu.VMEM((32, 8, RANK), F32),
             pltpu.VMEM((8, 64, RANK), F32),
@@ -378,7 +387,14 @@
             vmem_limit_bytes=56 * 2**20,
         ),
         name="cp_gradient",
-    )(values, weights, exps, coords, counts, uf, itf, cf)
+    )(values, weights, exps, jnp.transpose(coords, (0, 1, 4, 2, 3)), counts, uf, itf, cf)
+    return pl.pallas_call(
+        copy_out,
+        in_specs=[vmem] * 3,
+        out_specs=[vmem] * 3,
+        out_shape=[jax.ShapeDtypeStruct(g.shape, F32) for g in grads],
+        name="copy_out",
+    )(*grads)
 
 
 def solution(mesh):

time: 69.7 us -> 57.8 us (0.83)
  Pallas kernels: 62.6 us -> 56.3 us
  local copies, waits for them, and re-layouts: 5.5 us -> 0 us
    pallas_call x1, Pallas kernels: 62.6 us -> 54.8 us  [local(): pl.pallas_call(kernel, in_specs=[hbm, hbm, smem, smem, smem, vmem, vmem,...]
    unnamed x4 -> x0, local copies, waits for them, and re-layouts: 5.5 us -> none
    pallas_call x0 -> x1, Pallas kernels: none -> 1.51 us  [local(): pl.pallas_call(copy_out, in_specs=[vmem] * 3, out_specs=[vmem] * 3, out_s...]
where the time goes in v2:
time: 57.8 us; the launch traced here: 57.6 us
  Pallas kernels  56.3 us (97%)
  between operations  1.29 us (2%)
    pallas_call x1, Pallas kernels, local(): pl.pallas_call(kernel, in_specs=[hbm, hbm, smem, smem, smem, vmem, vmem,...  54.8 us
    pallas_call x1, Pallas kernels, local(): pl.pallas_call(copy_out, in_specs=[vmem] * 3, out_specs=[vmem] * 3, out_s...  1.51 us

profile of v2, /device:TPU:1, one launch (start us, length us, event | category | flops | bytes accessed | tf_op | source)
XLA Modules:
  0.0 57.6 jit_solution(4376745224980565275)
XLA Ops:
  1.3 54.8 %cp_gradient.1 = (f32[64,256]{1,0:T(8,128)}, f32[32,256]{1,0:T(8,128)}, f32[8,256]{1,0:T(8,128)}) custom-call(bf16[1,1,1,16,16,128,128]{6,5,4,3,2,1,0:T(8,128)(2,1)} %values.1, bf16[1,1,1,16,16,128,128]{6,5,4,3,2,1,0:T(8,128)(2,1)} %weights.1, s32[1,1,1,16]{3,2,1,0:T(1,128)} %exps.1, s32[1,1,3,1,16]{4,3,2,1,0:T(1,128)} %bitcast.1, ...), custom_call_target="tpu_custom_call" | custom-call | tf_op jit(solution)/shard_map/cp_gradient/pallas_call | solution.py:347
  56.0 1.5 %copy_out.1 = (f32[64,256]{1,0:T(8,128)}, f32[32,256]{1,0:T(8,128)}, f32[8,256]{1,0:T(8,128)}) custom-call(f32[64,256]{1,0:T(8,128)} %get-tuple-element.6.ug, f32[32,256]{1,0:T(8,128)} %get-tuple-element.7.ig, f32[8,256]{1,0:T(8,128)} %get-tuple-element.8.cg), custom_call_target="tpu_custom_call" | custom-call | tf_op jit(solution)/shard_map/copy_out/pallas_call | solution.py:391

commit v3 on v2

--- a/solution.py
+++ b/solution.py
@@ -28,6 +28,25 @@
 
 def wait_bytes(ref, sem):
     pltpu.make_async_copy(ref, ref, sem).wait()
+
+
+def pack(rows):
+    left, right = rows[:, :128], rows[:, 128:]
+    peak = jnp.max(jnp.maximum(jnp.abs(left), jnp.abs(right)), axis=0, keepdims=True)
+    power = jnp.floor(jnp.log2(jnp.maximum(peak, 2.0**-90))) + 1.0
+    scale = jnp.exp2(-power) * 32000.0
+    high = jnp.round(left * scale).astype(jnp.int32)
+    low = jnp.round(right * scale).astype(jnp.int32)
+    codes = lax.shift_left(high, 16) | (low & 0xFFFF)
+    return codes, power.astype(jnp.int32)
+
+
+def unpack(ref, j, n):
+    codes = ref[j, :n]
+    step = jnp.exp2(ref[j, n : n + 1].astype(F32)) * (1.0 / 32000.0)
+    high = lax.shift_right_arithmetic(codes, 16).astype(F32)
+    low = lax.shift_right_arithmetic(lax.shift_left(codes, 16), 16).astype(F32)
+    return jnp.concatenate([high * step, low * step], axis=1)
 
 
 def kernel(
@@ -60,6 +79,9 @@
     csum,
     umate,
     imate,
+    usend,
+    isend,
+    csend,
     urecv,
     irecv,
     crecv,
@@ -275,13 +297,24 @@
     user_mate.start()
 
     item_mate.wait()
-    for j in range(16):
-        imate[j] += isum[core, j]
-    irecv[ij] = imate[ij]
+
+    def pack_item(j, carry):
+        rows = imate[j] + isum[core, j]
+        imate[j] = rows
+        isend[j, :32], isend[j, 32:33] = pack(rows)
+        return carry
+
+    lax.fori_loop(0, 16, pack_item, 0, unroll=4)
 
     def scatter_item(d, carry):
         j = (ij + d) % 16
-        copy_to(imate.at[j], irecv.at[ij], rsend.at[3], rrecv.at[3], item_peer(d)).start()
+        copy_to(
+            isend.at[j, pl.ds(0, 33)],
+            irecv.at[ij, pl.ds(0, 33)],
+            rsend.at[3],
+            rrecv.at[3],
+            item_peer(d),
+        ).start()
         return carry
 
     lax.fori_loop(1, 16, scatter_item, 0)
@@ -289,39 +322,69 @@
     lax.fori_loop(0, SLOTS, functools.partial(phase_b, 1), 0, unroll=4)
 
     user_mate.wait()
-    for t in range(UT):
-        umate[t] += uterms[1, last[0, t]]
-    urecv[uj] = umate[uj]
+
+    def pack_user(j, carry):
+        rows = umate[j] + uterms[1, last[0, j]]
+        umate[j] = rows
+        usend[j, :64], usend[j, 64:65] = pack(rows)
+        return carry
+
+    lax.fori_loop(0, 8, pack_user, 0, unroll=4)
 
     def scatter_user(d, carry):
         j = (uj + d) % 8
-        copy_to(umate.at[j], urecv.at[uj], rsend.at[2], rrecv.at[2], user_peer(d)).start()
+        copy_to(
+            usend.at[j, pl.ds(0, 65)],
+            urecv.at[uj, pl.ds(0, 65)],
+            rsend.at[2],
+            rrecv.at[2],
+            user_peer(d),
+        ).start()
         return carry
 
     lax.fori_loop(1, 8, scatter_user, 0)
 
-    for t in range(CT):
+    def pack_ctx(t, carry):
         rows = cterms[0, last[2, t]] + cterms[1, last[2, t]]
         csum[2 * t] = rows[:8]
         csum[2 * t + 1] = rows[8:]
-    crecv[cj] = csum[cj]
+        csend[2 * t, :8], csend[2 * t, 8:9] = pack(rows[:8])
+        csend[2 * t + 1, :8], csend[2 * t + 1, 8:9] = pack(rows[8:])
+        return carry
+
+    lax.fori_loop(0, CT, pack_ctx, 0, unroll=4)
 
     def scatter_ctx(d, carry):
         j = (cj + d) % 32
-        copy_to(csum.at[j], crecv.at[cj], rsend.at[4], rrecv.at[4], ctx_peer(d)).start()
+        copy_to(
+            csend.at[j, pl.ds(0, 9)],
+            crecv.at[cj, pl.ds(0, 9)],
+            rsend.at[4],
+            rrecv.at[4],
+            ctx_peer(d),
+        ).start()
         return carry
 
     lax.fori_loop(1, 32, scatter_ctx, 0)
 
-    wait_bytes(irecv.at[pl.ds(0, 15)], rrecv.at[3])
-    ig_out[...] = jnp.sum(irecv[...], axis=0)
-    wait_bytes(urecv.at[pl.ds(0, 7)], rrecv.at[2])
-    ug_out[...] = jnp.sum(urecv[...], axis=0)
-    wait_bytes(crecv.at[pl.ds(0, 31)], rrecv.at[4])
-    cg_out[...] = jnp.sum(crecv[...], axis=0)
-    wait_bytes(urecv.at[pl.ds(0, 7)], rsend.at[2])
-    wait_bytes(irecv.at[pl.ds(0, 15)], rsend.at[3])
-    wait_bytes(crecv.at[pl.ds(0, 31)], rsend.at[4])
+    wait_bytes(irecv.at[pl.ds(0, 15), pl.ds(0, 33)], rrecv.at[3])
+    total = imate[ij]
+    for d in range(1, 16):
+        total = total + unpack(irecv, (ij + d) % 16, 32)
+    ig_out[...] = total
+    wait_bytes(urecv.at[pl.ds(0, 7), pl.ds(0, 65)], rrecv.at[2])
+    total = umate[uj]
+    for d in range(1, 8):
+        total = total + unpack(urecv, (uj + d) % 8, 64)
+    ug_out[...] = total
+    wait_bytes(crecv.at[pl.ds(0, 31), pl.ds(0, 9)], rrecv.at[4])
+    total = csum[cj]
+    for d in range(1, 32):
+        total = total + unpack(crecv, (cj + d) % 32, 8)
+    cg_out[...] = total
+    wait_bytes(urecv.at[pl.ds(0, 7), pl.ds(0, 65)], rsend.at[2])
+    wait_bytes(irecv.at[pl.ds(0, 15), pl.ds(0, 33)], rsend.at[3])
+    wait_bytes(crecv.at[pl.ds(0, 31), pl.ds(0, 9)], rsend.at[4])
 
 
 def copy_out(ug, ig, cg, ug_out, ig_out, cg_out):
@@ -372,9 +435,12 @@
             pltpu.VMEM((32, 8, RANK), F32),
             pltpu.VMEM((8, 64, RANK), F32),
             pltpu.VMEM((16, 32, RANK), F32),
-            pltpu.VMEM((8, 64, RANK), F32),
-            pltpu.VMEM((16, 32, RANK), F32),
-            pltpu.VMEM((32, 8, RANK), F32),
+            pltpu.VMEM((8, 72, 128), jnp.int32),
+            pltpu.VMEM((16, 40, 128), jnp.int32),
+            pltpu.VMEM((32, 16, 128), jnp.int32),
+            pltpu.VMEM((8, 72, 128), jnp.int32),
+            pltpu.VMEM((16, 40, 128), jnp.int32),
+            pltpu.VMEM((32, 16, 128), jnp.int32),
             dma((2, SLOTS)),
             dma((5,)),
             dma((5,)),

time: 57.8 us -> 52.4 us (0.907)
  Pallas kernels: 56.3 us -> 50.8 us
    pallas_call x1, Pallas kernels: 54.8 us -> 49.3 us  [local(): pl.pallas_call(kernel, in_specs=[hbm, hbm, smem, smem, smem, vmem, vmem,...]
where the time goes in v3:
time: 52.4 us; the launch traced here: 52.1 us
  Pallas kernels  50.8 us (97%)
  between operations  1.29 us (2%)
    pallas_call x1, Pallas kernels, local(): pl.pallas_call(kernel, in_specs=[hbm, hbm, smem, smem, smem, vmem, vmem,...  49.3 us
    pallas_call x1, Pallas kernels, local(): pl.pallas_call(copy_out, in_specs=[vmem] * 3, out_specs=[vmem] * 3, out_s...  1.51 us

profile of v3, /device:TPU:1, one launch (start us, length us, event | category | flops | bytes accessed | tf_op | source)
XLA Modules:
  0.0 52.1 jit_solution(5120212659904536177)
XLA Ops:
  1.3 49.3 %cp_gradient.1 = (f32[64,256]{1,0:T(8,128)}, f32[32,256]{1,0:T(8,128)}, f32[8,256]{1,0:T(8,128)}) custom-call(bf16[1,1,1,16,16,128,128]{6,5,4,3,2,1,0:T(8,128)(2,1)} %values.1, bf16[1,1,1,16,16,128,128]{6,5,4,3,2,1,0:T(8,128)(2,1)} %weights.1, s32[1,1,1,16]{3,2,1,0:T(1,128)} %exps.1, s32[1,1,3,1,16]{4,3,2,1,0:T(1,128)} %bitcast.1, ...), custom_call_target="tpu_custom_call" | custom-call | tf_op jit(solution)/shard_map/cp_gradient/pallas_call | solution.py:410
  50.6 1.5 %copy_out.1 = (f32[64,256]{1,0:T(8,128)}, f32[32,256]{1,0:T(8,128)}, f32[8,256]{1,0:T(8,128)}) custom-call(f32[64,256]{1,0:T(8,128)} %get-tuple-element.6.ug, f32[32,256]{1,0:T(8,128)} %get-tuple-element.7.ig, f32[8,256]{1,0:T(8,128)} %get-tuple-element.8.cg), custom_call_target="tpu_custom_call" | custom-call | tf_op jit(solution)/shard_map/copy_out/pallas_call | solution.py:457

commit v4 on v3

--- a/solution.py
+++ b/solution.py
@@ -41,9 +41,8 @@
     return codes, power.astype(jnp.int32)
 
 
-def unpack(ref, j, n):
-    codes = ref[j, :n]
-    step = jnp.exp2(ref[j, n : n + 1].astype(F32)) * (1.0 / 32000.0)
+def unpack(codes, power):
+    step = jnp.exp2(power.astype(F32)) * (1.0 / 32000.0)
     high = lax.shift_right_arithmetic(codes, 16).astype(F32)
     low = lax.shift_right_arithmetic(lax.shift_left(codes, 16), 16).astype(F32)
     return jnp.concatenate([high * step, low * step], axis=1)
@@ -116,8 +115,6 @@
             copy.start()
         return carry
 
-    lax.fori_loop(0, SLOTS, start_load, 0)
-
     def user_peer(d):
         j = (uj + d) % 8
         return (u, j // 2, (j % 2) * 2 + core)
@@ -143,6 +140,23 @@
     greet(item_peer, 16)
     greet(ctx_peer, 32)
     pl.semaphore_signal(barrier, inc=1, device_id=mate, device_id_type=MESH)
+
+    pl.semaphore_wait(barrier, 7 + 15 + 31 + 1)
+
+    def gather_user(d, carry):
+        copy_to(uf, ublk.at[core, uj], gsend.at[0], grecv.at[0], user_peer(d)).start()
+        return carry
+
+    def gather_item(d, carry):
+        copy_to(itf, iblk.at[core, ij], gsend.at[1], grecv.at[1], item_peer(d)).start()
+        return carry
+
+    def gather_ctx(d, carry):
+        copy_to(cstage, cblk.at[cj], gsend.at[2], grecv.at[2], ctx_peer(d)).start()
+        return carry
+
+    lax.fori_loop(1, 16, gather_item, 0)
+    lax.fori_loop(1, 8, gather_user, 0)
 
     ublk[core, uj] = uf[...]
     iblk[core, ij] = itf[...]
@@ -150,23 +164,8 @@
     cstage[...] = jnp.concatenate([own[:, :128], own[:, 128:]], axis=0).astype(BF16)
     cblk[cj] = cstage[...]
 
-    pl.semaphore_wait(barrier, 7 + 15 + 31 + 1)
-
-    def gather_user(d, carry):
-        copy_to(uf, ublk.at[core, uj], gsend.at[0], grecv.at[0], user_peer(d)).start()
-        return carry
-
-    def gather_item(d, carry):
-        copy_to(itf, iblk.at[core, ij], gsend.at[1], grecv.at[1], item_peer(d)).start()
-        return carry
-
-    def gather_ctx(d, carry):
-        copy_to(cstage, cblk.at[cj], gsend.at[2], grecv.at[2], ctx_peer(d)).start()
-        return carry
-
-    lax.fori_loop(1, 16, gather_item, 0)
-    lax.fori_loop(1, 8, gather_user, 0)
     lax.fori_loop(1, 32, gather_ctx, 0)
+    lax.fori_loop(0, SLOTS, start_load, 0)
 
     count = counts[0, 0, 0]
     tile = [[coords[0, 0, m, 0, s] for s in range(SLOTS)] for m in range(3)]
@@ -243,7 +242,6 @@
         scale = lax.shift_left(jnp.int32(1), exps[0, 0, 0, slot] + 30).astype(F32) * (
             2.0**-30
         )
-        term = jnp.zeros((TI, RANK), F32)
         for k in range(0, DEPTH, step):
             ag = (a[None] * g[k : k + step][:, None, :]).reshape(step * TU, RANK)
             model = lax.dot_general(
@@ -255,6 +253,19 @@
             for n in range(step):
                 errs[slot, 0, k + n] = err[n * TU : n * TU + 64]
                 errs[slot, 1, k + n] = err[n * TU + 64 : n * TU + TU]
+        return carry
+
+    def phase_item(slot, carry):
+        t = coords[0, 0, 0, 0, slot]
+        a = jnp.concatenate([ublk[0, t], ublk[1, t]], axis=0)
+        g = gblk[coords[0, 0, 2, 0, slot]].astype(BF16)
+        term = jnp.zeros((TI, RANK), F32)
+        for k in range(0, DEPTH, step):
+            ag = (a[None] * g[k : k + step][:, None, :]).reshape(step * TU, RANK)
+            err = jnp.concatenate(
+                [errs[slot, half, k + n] for n in range(step) for half in range(2)],
+                axis=0,
+            )
             term = term + lax.dot_general(
                 err, ag, (((0,), (0,)), ((), ())), preferred_element_type=F32
             )
@@ -279,6 +290,7 @@
         return carry
 
     lax.fori_loop(0, SLOTS, phase_a, 0, unroll=4)
+    lax.fori_loop(0, SLOTS, phase_item, 0, unroll=4)
 
     for t in range(IT):
         rows = iterms[last[1, t]]
@@ -289,12 +301,8 @@
     item_mate = copy_to(isum.at[1 - core], imate, rsend.at[1], rrecv.at[1], mate)
     item_mate.start()
 
-    lax.fori_loop(0, SLOTS, functools.partial(phase_b, 0), 0, unroll=4)
-
-    for t in range(UT):
-        usum[t] = uterms[0, last[0, t]]
-    user_mate = copy_to(usum, umate, rsend.at[0], rrecv.at[0], mate)
-    user_mate.start()
+    early = SLOTS // 2
+    lax.fori_loop(0, early, functools.partial(phase_b, 0), 0, unroll=4)
 
     item_mate.wait()
 
@@ -319,7 +327,37 @@
 
     lax.fori_loop(1, 16, scatter_item, 0)
 
+    lax.fori_loop(early, SLOTS, functools.partial(phase_b, 0), 0, unroll=4)
+
+    for t in range(UT):
+        usum[t] = uterms[0, last[0, t]]
+    user_mate = copy_to(usum, umate, rsend.at[0], rrecv.at[0], mate)
+    user_mate.start()
+
     lax.fori_loop(0, SLOTS, functools.partial(phase_b, 1), 0, unroll=4)
+
+    def pack_ctx(t, carry):
+        rows = cterms[0, last[2, t]] + cterms[1, last[2, t]]
+        csum[2 * t] = rows[:8]
+        csum[2 * t + 1] = rows[8:]
+        csend[2 * t, :8], csend[2 * t, 8:9] = pack(rows[:8])
+        csend[2 * t + 1, :8], csend[2 * t + 1, 8:9] = pack(rows[8:])
+        return carry
+
+    lax.fori_loop(0, CT, pack_ctx, 0, unroll=4)
+
+    def scatter_ctx(d, carry):
+        j = (cj + d) % 32
+        copy_to(
+            csend.at[j, pl.ds(0, 9)],
+            crecv.at[cj, pl.ds(0, 9)],
+            rsend.at[4],
+            rrecv.at[4],
+            ctx_peer(d),
+        ).start()
+        return carry
+
+    lax.fori_loop(1, 32, scatter_ctx, 0)
 
     user_mate.wait()
 
@@ -344,43 +382,23 @@
 
     lax.fori_loop(1, 8, scatter_user, 0)
 
-    def pack_ctx(t, carry):
-        rows = cterms[0, last[2, t]] + cterms[1, last[2, t]]
-        csum[2 * t] = rows[:8]
-        csum[2 * t + 1] = rows[8:]
-        csend[2 * t, :8], csend[2 * t, 8:9] = pack(rows[:8])
-        csend[2 * t + 1, :8], csend[2 * t + 1, 8:9] = pack(rows[8:])
-        return carry
-
-    lax.fori_loop(0, CT, pack_ctx, 0, unroll=4)
-
-    def scatter_ctx(d, carry):
-        j = (cj + d) % 32
-        copy_to(
-            csend.at[j, pl.ds(0, 9)],
-            crecv.at[cj, pl.ds(0, 9)],
-            rsend.at[4],
-            rrecv.at[4],
-            ctx_peer(d),
-        ).start()
-        return carry
-
-    lax.fori_loop(1, 32, scatter_ctx, 0)
-
     wait_bytes(irecv.at[pl.ds(0, 15), pl.ds(0, 33)], rrecv.at[3])
     total = imate[ij]
     for d in range(1, 16):
-        total = total + unpack(irecv, (ij + d) % 16, 32)
+        j = (ij + d) % 16
+        total = total + unpack(irecv[j, :32], irecv[j, 32:33])
     ig_out[...] = total
     wait_bytes(urecv.at[pl.ds(0, 7), pl.ds(0, 65)], rrecv.at[2])
     total = umate[uj]
     for d in range(1, 8):
-        total = total + unpack(urecv, (uj + d) % 8, 64)
+        j = (uj + d) % 8
+        total = total + unpack(urecv[j, :64], urecv[j, 64:65])
     ug_out[...] = total
     wait_bytes(crecv.at[pl.ds(0, 31), pl.ds(0, 9)], rrecv.at[4])
     total = csum[cj]
     for d in range(1, 32):
-        total = total + unpack(crecv, (cj + d) % 32, 8)
+        j = (cj + d) % 32
+        total = total + unpack(crecv[j, :8], crecv[j, 8:9])
     cg_out[...] = total
     wait_bytes(urecv.at[pl.ds(0, 7), pl.ds(0, 65)], rsend.at[2])
     wait_bytes(irecv.at[pl.ds(0, 15), pl.ds(0, 33)], rsend.at[3])

time: 52.4 us -> 50.2 us (0.958)
  Pallas kernels: 50.8 us -> 48.7 us
    pallas_call x1, Pallas kernels: 49.3 us -> 47.2 us  [local(): pl.pallas_call(kernel, in_specs=[hbm, hbm, smem, smem, smem, vmem, vmem,...]
where the time goes in v4:
time: 50.2 us; the launch traced here: 49.9 us
  Pallas kernels  48.7 us (97%)
  between operations  1.29 us (3%)
    pallas_call x1, Pallas kernels, local(): pl.pallas_call(kernel, in_specs=[hbm, hbm, smem, smem, smem, vmem, vmem,...  47.2 us
    pallas_call x1, Pallas kernels, local(): pl.pallas_call(copy_out, in_specs=[vmem] * 3, out_specs=[vmem] * 3, out_s...  1.51 us

profile of v4, /device:TPU:1, one launch (start us, length us, event | category | flops | bytes accessed | tf_op | source)
XLA Modules:
  0.0 49.9 jit_solution(14907753562684277303)
XLA Ops:
  1.3 47.2 %cp_gradient.1 = (f32[64,256]{1,0:T(8,128)}, f32[32,256]{1,0:T(8,128)}, f32[8,256]{1,0:T(8,128)}) custom-call(bf16[1,1,1,16,16,128,128]{6,5,4,3,2,1,0:T(8,128)(2,1)} %values.1, bf16[1,1,1,16,16,128,128]{6,5,4,3,2,1,0:T(8,128)(2,1)} %weights.1, s32[1,1,1,16]{3,2,1,0:T(1,128)} %exps.1, s32[1,1,3,1,16]{4,3,2,1,0:T(1,128)} %bitcast.1, ...), custom_call_target="tpu_custom_call" | custom-call | tf_op jit(solution)/shard_map/cp_gradient/pallas_call | solution.py:428
  48.4 1.5 %copy_out.1 = (f32[64,256]{1,0:T(8,128)}, f32[32,256]{1,0:T(8,128)}, f32[8,256]{1,0:T(8,128)}) custom-call(f32[64,256]{1,0:T(8,128)} %get-tuple-element.6.ug, f32[32,256]{1,0:T(8,128)} %get-tuple-element.7.ig, f32[8,256]{1,0:T(8,128)} %get-tuple-element.8.cg), custom_call_target="tpu_custom_call" | custom-call | tf_op jit(solution)/shard_map/copy_out/pallas_call | solution.py:475

commit v5 on v4

--- a/solution.py
+++ b/solution.py
@@ -289,7 +289,7 @@
         )
         return carry
 
-    lax.fori_loop(0, SLOTS, phase_a, 0, unroll=4)
+    lax.fori_loop(0, SLOTS, phase_a, 0, unroll=8)
     lax.fori_loop(0, SLOTS, phase_item, 0, unroll=4)
 
     for t in range(IT):

time: 50.2 us -> 49.8 us (level)
  no operation moved by 1% of the time
where the time goes in v5:
time: 49.8 us; the launch traced here: 49.6 us
  Pallas kernels  48.3 us (97%)
  between operations  1.29 us (3%)
    pallas_call x1, Pallas kernels, local(): pl.pallas_call(kernel, in_specs=[hbm, hbm, smem, smem, smem, vmem, vmem,...  46.8 us
    pallas_call x1, Pallas kernels, local(): pl.pallas_call(copy_out, in_specs=[vmem] * 3, out_specs=[vmem] * 3, out_s...  1.51 us

profile of v5, /device:TPU:1, one launch (start us, length us, event | category | flops | bytes accessed | tf_op | source)
XLA Modules:
  0.0 49.6 jit_solution(10304781000597012505)
XLA Ops:
  1.3 46.8 %cp_gradient.1 = (f32[64,256]{1,0:T(8,128)}, f32[32,256]{1,0:T(8,128)}, f32[8,256]{1,0:T(8,128)}) custom-call(bf16[1,1,1,16,16,128,128]{6,5,4,3,2,1,0:T(8,128)(2,1)} %values.1, bf16[1,1,1,16,16,128,128]{6,5,4,3,2,1,0:T(8,128)(2,1)} %weights.1, s32[1,1,1,16]{3,2,1,0:T(1,128)} %exps.1, s32[1,1,3,1,16]{4,3,2,1,0:T(1,128)} %bitcast.1, ...), custom_call_target="tpu_custom_call" | custom-call | tf_op jit(solution)/shard_map/cp_gradient/pallas_call | solution.py:428
  48.1 1.5 %copy_out.1 = (f32[64,256]{1,0:T(8,128)}, f32[32,256]{1,0:T(8,128)}, f32[8,256]{1,0:T(8,128)}) custom-call(f32[64,256]{1,0:T(8,128)} %get-tuple-element.6.ug, f32[32,256]{1,0:T(8,128)} %get-tuple-element.7.ig, f32[8,256]{1,0:T(8,128)} %get-tuple-element.8.cg), custom_call_target="tpu_custom_call" | custom-call | tf_op jit(solution)/shard_map/copy_out/pallas_call | solution.py:475
